TPU v7x, 32 devices: a whole 2x2x4 slice. The times are simulated.
32 devices in a mesh: enc: 8 (over y, x, core), rep: 4 (over z).
Axes of the slice: x: 2, y: 2, z: 4, core: 2. Of those that a mesh axis runs over, the one named last changes fastest.
Arguments:
- pixels: bfloat16 [4096, 1280], P(('enc', 'rep')), may hold values from -6 to 6
- window_owner: int32 [256], P(('enc', 'rep')), may hold values from 0 to 7, as said below
- window_len: int32 [256], P(('enc', 'rep')), may hold values from 4 to 16, as said below
- slot_token: int32 [5120], P(('enc', 'rep')), may hold values from -1 to 31, as said below
- cotangent: bfloat16 [5120, 5120], P(('enc', 'rep')), may hold values from -6 to 6
- w_qkv: bfloat16 [1280, 1920], replicated
- w_out: bfloat16 [640, 1280], replicated, may hold values from -0.25 to 0.25
- gain: float32 [1280], replicated, may hold values from 0.1 to 1.9
Outputs:
- embeddings: bfloat16 [5120, 5120], P(('enc', 'rep'))
- grad_w_out: float32 [640, 1280], P('enc')
Inputs may be any that keep to these rules, and one draw needn't show every extreme that they name: `window_owner`: the 8 windows of one device name distinct owners, taken in the device's own rep group; in each rep group one owner is named by a window of every device. `window_len`: A multiple of 4. `slot_token`: on the device of enc index o and rep index r, the value 4 * s + m names merged token m of the window that the device of enc index s and rep index r sends to o. Each such value appears exactly once, for every m < window_len / 4 of that window and for no other m; -1 marks other tokens. The merged tokens of one window stand in consecutive rows in order, wrapping around at the end of the device's rows.
All inputs are finite; a program needn't handle non-finite values.
Results may differ from a plain program's by a relative error of at most 0.012.
The roundings to bfloat16 on the way count: a program that leaves them out, or rounds other values in their place, can miss the bound.
Values may be sent and summed in bfloat16 or wider, within the bound.
No kernel may reach another device: no remote copies, remote signals or barrier semaphores. Data moves between devices by JAX's collectives and lax.ppermute only.
A program may use at most 64 MiB of HBM per device.

v0:
```python
import math
import jax
import jax.numpy as jnp
from jax import lax
from jax.sharding import PartitionSpec as P

HD = 80
HEADS = 8
MERGE = 4


def normalize(inputs, gain):
    values = inputs.astype(jnp.float32)
    mean_square = jnp.mean(values * values, axis=-1, keepdims=True)
    return (values * lax.rsqrt(mean_square + 1e-06) * gain).astype(jnp.bfloat16)


def encode(windows, lengths, w_qkv, w_out, gain):
    number, window_size, feature_width = windows.shape
    inner_width = w_out.shape[0]
    flat_rows = windows.reshape(number * window_size, feature_width)
    normed = normalize(flat_rows, gain)
    projected = jnp.dot(normed, w_qkv, preferred_element_type=jnp.float32).astype(jnp.bfloat16)
    queries = projected[:, :inner_width].reshape(number, window_size, HEADS, HD)
    keys_all = projected[:, inner_width : 2 * inner_width].reshape(number, window_size, HEADS, HD)
    values_all = projected[:, 2 * inner_width :].reshape(number, window_size, HEADS, HD)
    scores = jnp.einsum(
        "nqhd,nkhd->nhqk", queries, keys_all, preferred_element_type=jnp.float32
    ) / math.sqrt(HD)
    live_keys = jnp.arange(window_size, dtype=jnp.int32)[None, :] < lengths[:, None]
    scores = jnp.where(live_keys[:, None, None, :], scores, -1e30)
    weights = jax.nn.softmax(scores, axis=-1).astype(jnp.bfloat16)
    attended = jnp.einsum(
        "nhqk,nkhd->nqhd", weights, values_all, preferred_element_type=jnp.float32
    )
    attended = attended.astype(jnp.bfloat16).reshape(number * window_size, inner_width)
    encoded = flat_rows.astype(jnp.float32) + jnp.dot(
        attended, w_out, preferred_element_type=jnp.float32
    )
    return (encoded.astype(jnp.bfloat16), attended)


def shards(pixels, window_owner, window_len, slot_token, cotangent, w_qkv, w_out, gain):
    group_size = lax.axis_size("enc")
    replica_count = lax.axis_size("rep")
    feature_width = pixels.shape[1]
    window_count = window_owner.shape[0]
    window_rows = pixels.shape[0] // window_count
    tokens_each = window_rows // MERGE
    merged_width = MERGE * feature_width
    owner_ids = jnp.arange(group_size, dtype=jnp.int32)
    route = (window_owner[None, :] == owner_ids[:, None]).astype(jnp.bfloat16)
    slot_ids = jnp.arange(group_size * tokens_each, dtype=jnp.int32)
    placing = (slot_token[:, None] == slot_ids[None, :]).astype(jnp.bfloat16)
    encoded, attended = encode(
        pixels.reshape(window_count, window_rows, feature_width), window_len, w_qkv, w_out, gain
    )
    outgoing = jnp.dot(
        route,
        encoded.reshape(window_count, window_rows * feature_width),
        preferred_element_type=jnp.float32,
    )
    outgoing = outgoing.astype(jnp.bfloat16).reshape(group_size, tokens_each, merged_width)
    arrived = lax.all_to_all(outgoing, "enc", split_axis=0, concat_axis=0, tiled=True)
    embeddings = jnp.dot(
        placing,
        arrived.reshape(group_size * tokens_each, merged_width),
        preferred_element_type=jnp.float32,
    ).astype(jnp.bfloat16)
    returning = lax.dot_general(
        placing, cotangent, (((0,), (0,)), ((), ())), preferred_element_type=jnp.float32
    )
    returning = returning.astype(jnp.bfloat16).reshape(group_size, tokens_each, merged_width)
    answered = lax.all_to_all(returning, "enc", split_axis=0, concat_axis=0, tiled=True)
    d_encoded = lax.dot_general(
        route,
        answered.reshape(group_size, tokens_each * merged_width),
        (((0,), (0,)), ((), ())),
        preferred_element_type=jnp.float32,
    )
    d_encoded = d_encoded.astype(jnp.bfloat16).reshape(window_count * window_rows, feature_width)
    reduced = lax.psum_scatter(
        lax.dot_general(
            attended, d_encoded, (((0,), (0,)), ((), ())), preferred_element_type=jnp.float32
        ),
        "enc",
        scatter_dimension=0,
        tiled=True,
    )
    summed = lax.psum(reduced, "rep")
    patch_total = window_count * window_rows * group_size * replica_count
    gradient = summed / math.sqrt(patch_total)
    return (embeddings, gradient)


def solution(mesh):
    return jax.shard_map(
        shards,
        mesh=mesh,
        in_specs=(
            P(("enc", "rep"), None),
            P(("enc", "rep")),
            P(("enc", "rep")),
            P(("enc", "rep")),
            P(("enc", "rep"), None),
            P(),
            P(),
            P(),
        ),
        out_specs=(P(("enc", "rep"), None), P("enc", None)),
        check_vma=False,
    )
```

profile of v0, /device:TPU:0, one launch (start us, length us, event | category | flops | bytes accessed | tf_op | source)
XLA Modules:
  0.0 123.2 jit_solution(14460333167618268343)
XLA Ops:
  7.2 0.0 copy-start
  7.2 0.0 copy-start.1
  7.2 0.0 copy-start.2
  7.2 1.4 %copy-done = bf16[160,5120]{1,0:T(8,128)(2,1)S(1)} copy-done((bf16[160,5120]{1,0:T(8,128)(2,1)S(1)}, bf16[160,5120]{1,0:T(8,128)(2,1)}, u32[]{:S(2)}) %copy-start) | copy-done | bytes 1638424
  8.6 1.1 convolution_convert_fusion.3
  9.7 0.9 reshape.71
  10.6 5.2 %all-to-all-start.1 = ((bf16[8,4,5120]{2,1,0:T(4,128)(2,1)}), bf16[8,4,5120]{2,1,0:T(4,128)(2,1)S(1)}, u32[]{:S(2)}, u32[]{:S(2)}) async-start(bf16[8,4,5120]{2,1,0:T(4,128)(2,1)} %reshape.71), calls=%async_computation.1 | async-start | bytes 655360 | tf_op jit(solution)/shard_map/all_to_all | solution.py:74
  15.8 0.0 reduce-scatter.2.cloned.1.call-start
  15.8 0.0 copy-done.1
  15.8 0.1 fusion.6
  16.0 0.0 copy-done.2
  16.0 3.3 %convolution_convert_fusion.4 = bf16[128,1920]{1,0:T(8,128)(2,1)S(1)} fusion(bf16[1280,1920]{1,0:T(8,128)(2,1)} %param.13, bf16[128,1280]{1,0:T(8,128)(2,1)S(1)} %copy-done.1, f32[1280]{0:T(1024)S(1)} %copy-done.2, f32[128]{0:T(128)S(1)} %add_rsqrt_fusion), kind=kOutput, calls=%fused_computation.7 | convolution fusion | flops 630046720 | bytes 5740032 | tf_op jit(solution)/shard_map/dot_general | solution.py:23
  19.4 0.0 copy-start.5
  19.4 0.3 reshape.65
  19.7 0.3 reshape.66
  20.0 0.0 copy-done.5
  20.0 0.1 iota_compare_fusion.3
  20.1 1.1 fusion.4
  21.2 0.4 fusion.26
  21.6 0.3 reshape.64
  21.8 0.0 copy-start.4
  21.8 1.6 %fusion.5 = bf16[8,16,8,80]{3,1,2,0:T(8,128)(2,1)S(1)} fusion(bf16[8,16,8,80]{3,2,1,0:T(8,128)(2,1)S(1)} %reshape.64, f32[8,8,16]{2,1,0:T(8,128)S(1)} %fusion.26, f32[8,8,16,16]{2,3,1,0:T(8,128)} %fusion.4), kind=kOutput, calls=%fused_computation.13 | convolution fusion | flops 2753551 | bytes 397312 | tf_op jit(solution)/shard_map/nhqk,nkhd->nqhd/dot_general | solution.py:33
  23.4 0.1 copy.18
  23.5 0.2 reshape.67
  23.7 0.0 all-to-all-done.1
  23.7 0.1 copy.21
  23.8 0.0 copy-done.4
  23.8 0.3 convolution_convert_fusion
  24.1 0.2 reshape.73
  24.3 2.3 %fusion.31 = f32[640,1280]{1,0:T(8,128)} fusion(bf16[128,640]{1,0:T(8,128)(2,1)S(1)} %reshape.67, bf16[128,1280]{1,0:T(8,128)(2,1)S(1)} %reshape.73), kind=kOutput, calls=%fused_computation.38 | convolution fusion | flops 209715200 | bytes 3768320 | tf_op jit(solution)/shard_map/dot_general | solution.py:83
  26.6 0.0 reduce-scatter.2.cloned.1.call-update
  26.6 1.9 %fusion.1 = bf16[128,1280]{1,0:T(8,128)(2,1)S(1)} fusion(bf16[128,640]{1,0:T(8,128)(2,1)S(1)} %reshape.67, bf16[640,1280]{1,0:T(8,128)(2,1)} %param.14, bf16[128,1280]{1,0:T(8,128)(2,1)S(1)} %copy-done.1), kind=kOutput, calls=%fused_computation.6 | convolution fusion | flops 210206720 | bytes 2457600 | tf_op jit(solution)/shard_map/dot_general | solution.py:37
  28.5 0.2 reshape.68
  28.7 0.0 copy-start.3
  28.7 0.2 convolution_convert_fusion.1
  28.9 1.0 copy.19
  29.9 4.2 %all-to-all-start = ((bf16[8,4,5120]{2,1,0:T(4,128)(2,1)}), bf16[8,4,5120]{2,1,0:T(4,128)(2,1)S(1)}, u32[]{:S(2)}, u32[]{:S(2)}) async-start(bf16[8,4,5120]{2,1,0:T(4,128)(2,1)} %copy.19), calls=%async_computation | async-start | bytes 655360 | tf_op jit(solution)/shard_map/all_to_all | solution.py:64
  34.1 0.0 all-reduce.2.cloned.1.call-start
  34.1 41.2 %reduce-scatter.2.cloned.1.call-done = f32[80,1280]{1,0:T(8,128)} async-done(((f32[640,1280]{1,0:T(8,128)}), f32[80,1280]{1,0:T(8,128)}) %reduce-scatter.2.cloned.1.call-update) | async-done | bytes 409616 | tf_op jit(solution)/shard_map/reduce_scatter | solution.py:82
  75.3 0.0 all-reduce.2.cloned.1.call-update
  75.3 0.0 all-to-all-done
  75.4 0.1 reshape.70
  75.4 0.0 copy-done.3
  75.4 1.8 %convolution_convert_fusion.2 = bf16[160,5120]{1,0:T(8,128)(2,1)} fusion(bf16[32,5120]{1,0:T(8,128)(2,1)S(1)} %reshape.70, s32[160]{0:T(256)S(1)} %copy-done.3), kind=kOutput, calls=%fused_computation.3 | convolution fusion | flops 53253120 | bytes 1966720 | tf_op jit(solution)/shard_map/dot_general | solution.py:65
  77.2 37.3 %all-reduce.2.cloned.1.call-done = f32[80,1280]{1,0:T(8,128)} async-done(((f32[80,1280]{1,0:T(8,128)}), f32[80,1280]{1,0:T(8,128)}) %all-reduce.2.cloned.1.call-update) | async-done | bytes 409616 | tf_op jit(solution)/shard_map/psum | solution.py:90
  114.6 1.8 %broadcast_multiply_fusion = f32[80,1280]{1,0:T(8,128)} fusion(f32[80,1280]{1,0:T(8,128)} %all-reduce.2.cloned.1.call-done), kind=kLoop, calls=%fused_computation.26 | loop fusion | flops 102400 | bytes 819200 | tf_op jit(solution)/shard_map/div | solution.py:92
  (2 shorter events, 0.1 us)
Async XLA Ops:
  7.2 1.4 %copy-start = (bf16[160,5120]{1,0:T(8,128)(2,1)S(1)}, bf16[160,5120]{1,0:T(8,128)(2,1)}, u32[]{:S(2)}) copy-start(bf16[160,5120]{1,0:T(8,128)(2,1)} %param.12) | copy-start | bytes 4915204
  7.2 8.7 %copy-start.1 = (bf16[128,1280]{1,0:T(8,128)(2,1)S(1)}, bf16[128,1280]{1,0:T(8,128)(2,1)}, u32[]{:S(2)}) copy-start(bf16[128,1280]{1,0:T(8,128)(2,1)} %param.8) | copy-start | bytes 983044
  7.2 8.8 %copy-start.2 = (f32[1280]{0:T(1024)S(1)}, f32[1280]{0:T(1024)}, u32[]{:S(2)}) copy-start(f32[1280]{0:T(1024)} %param.15) | copy-start | bytes 15364
  10.6 13.1 %all-to-all-start.1 = ((bf16[8,4,5120]{2,1,0:T(4,128)(2,1)}), bf16[8,4,5120]{2,1,0:T(4,128)(2,1)S(1)}, u32[]{:S(2)}, u32[]{:S(2)}) async-start(bf16[8,4,5120]{2,1,0:T(4,128)(2,1)} %reshape.71), calls=%async_computation.1 | async-start | bytes 655360 | tf_op jit(solution)/shard_map/all_to_all | solution.py:74
  15.8 59.5 %reduce-scatter.2.cloned.1.call-start = ((), (), s32[]{:S(2)}) async-start(), calls=%async_computation.3 | async-start | bytes 3686400 | tf_op jit(solution)/shard_map/reduce_scatter | solution.py:82
  19.4 0.7 copy-start.5
  21.8 2.0 %copy-start.4 = (s32[8]{0:T(128)S(1)}, s32[8]{0:T(128)}, u32[]{:S(2)}) copy-start(s32[8]{0:T(128)} %param.9) | copy-start | bytes 100
  28.7 46.8 %copy-start.3 = (s32[160]{0:T(256)S(1)}, s32[160]{0:T(256)}, u32[]{:S(2)}) copy-start(s32[160]{0:T(256)} %param.11) | copy-start | bytes 1924
  29.9 45.4 %all-to-all-start = ((bf16[8,4,5120]{2,1,0:T(4,128)(2,1)}), bf16[8,4,5120]{2,1,0:T(4,128)(2,1)S(1)}, u32[]{:S(2)}, u32[]{:S(2)}) async-start(bf16[8,4,5120]{2,1,0:T(4,128)(2,1)} %copy.19), calls=%async_computation | async-start | bytes 655360 | tf_op jit(solution)/shard_map/all_to_all | solution.py:64
  34.1 80.5 %all-reduce.2.cloned.1.call-start = ((), (), s32[]{:S(2)}) async-start(), calls=%async_computation.4 | async-start | bytes 819200 | tf_op jit(solution)/shard_map/psum | solution.py:90
Sparse Core Ops, SparseCore 0:
  26.7 48.5 reduce-scatter.1
  77.7 36.8 all-reduce.1
where the time goes:
time: 124 us; the launch traced here: 123 us
  waiting for transfers between devices  78.6 us (63%)
  between operations  14.2 us (11%)
  matrix products  14 us (11%)
  starting transfers between devices  9.41 us (8%)
  local copies, waits for them, and re-layouts  4.93 us (4%)
  other arithmetic  2.01 us (2%)
    reduce_scatter x1, waiting for transfers between devices, shards(): lax.psum_scatter(lax.dot_general(attended, d_encoded, (((0,), (0,)), ((),...  41.2 us
    psum x1, waiting for transfers between devices, shards(): summed = lax.psum(reduced, 'rep')  37.3 us
    all_to_all x1, starting transfers between devices, shards(): lax.all_to_all(returning, 'enc', split_axis=0, concat_axis=0, tiled=True)  5.18 us
    all_to_all x1, starting transfers between devices, shards(): lax.all_to_all(outgoing, 'enc', split_axis=0, concat_axis=0, tiled=True)  4.16 us
    dot_general x1, matrix products, encode(): jnp.dot(normed, w_qkv, preferred_element_type=jnp.float32)  3.35 us
  transfers between devices with their start and end apart: 4, of which 2 were waited for; matrix products, arithmetic and copies ran while one was open for 10% of the time, Pallas kernels for 0%

commit v1 on v0

--- a/solution.py
+++ b/solution.py
@@ -87,7 +87,9 @@
         scatter_dimension=0,
         tiled=True,
     )
-    summed = lax.psum(reduced, "rep")
+    summed = reduced
+    for hop in (1, 2):
+        summed = summed + lax.ppermute(summed, "rep", [(dev, dev ^ hop) for dev in range(4)])
     patch_total = window_count * window_rows * group_size * replica_count
     gradient = summed / math.sqrt(patch_total)
     return (embeddings, gradient)

time: 124 us -> 115 us (0.927)
  waiting for transfers between devices: 78.6 us -> 67.7 us
  starting transfers between devices: 9.41 us -> 12.6 us
    psum x1 -> x0, waiting for transfers between devices: 37.3 us -> none  [shards(): summed = lax.psum(reduced, 'rep')]
    ppermute x0 -> x2, waiting for transfers between devices: none -> 17.1 us  [shards(): lax.ppermute(summed, 'rep', [(dev, dev ^ hop) for dev in range(4)])]
    reduce_scatter x1, waiting for transfers between devices: 41.2 us -> 48.7 us  [shards(): lax.psum_scatter(lax.dot_general(attended, d_encoded, (((0,), (0,)), ((),...]
    ppermute x0 -> x2, starting transfers between devices: none -> 3.95 us  [shards(): lax.ppermute(summed, 'rep', [(dev, dev ^ hop) for dev in range(4)])]
    all_to_all x1, waiting for transfers between devices: 0.01 us -> 1.84 us  [shards(): lax.all_to_all(outgoing, 'enc', split_axis=0, concat_axis=0, tiled=True)]
  transfers between devices with their start and end apart: 4 -> 5, of which waited for: 2 -> 4; matrix products, arithmetic and copies ran while one was open for 10% -> 11% of each run, Pallas kernels for 0% -> 0%
where the time goes in v1:
time: 115 us; the launch traced here: 114 us
  waiting for transfers between devices  67.7 us (59%)
  between operations  14.2 us (12%)
  matrix products  14 us (12%)
  starting transfers between devices  12.6 us (11%)
  local copies, waits for them, and re-layouts  4.93 us (4%)
    reduce_scatter x1, waiting for transfers between devices, shards(): lax.psum_scatter(lax.dot_general(attended, d_encoded, (((0,), (0,)), ((),...  48.7 us
    ppermute x2, waiting for transfers between devices, shards(): lax.ppermute(summed, 'rep', [(dev, dev ^ hop) for dev in range(4)])  17.1 us
    all_to_all x1, starting transfers between devices, shards(): lax.all_to_all(returning, 'enc', split_axis=0, concat_axis=0, tiled=True)  5.18 us
    ppermute x2, starting transfers between devices, shards(): lax.ppermute(summed, 'rep', [(dev, dev ^ hop) for dev in range(4)])  3.95 us
    all_to_all x1, starting transfers between devices, shards(): lax.all_to_all(outgoing, 'enc', split_axis=0, concat_axis=0, tiled=True)  3.43 us
    dot_general x1, matrix products, encode(): jnp.dot(normed, w_qkv, preferred_element_type=jnp.float32)  3.35 us
  transfers between devices with their start and end apart: 5, of which 4 were waited for; matrix products, arithmetic and copies ran while one was open for 11% of the time, Pallas kernels for 0%

profile of v1, /device:TPU:0, one launch (start us, length us, event | category | flops | bytes accessed | tf_op | source)
XLA Modules:
  0.0 114.5 jit_solution(5075804860078853450)
XLA Ops:
  7.2 0.0 copy-start
  7.2 0.0 copy-start.1
  7.2 0.0 copy-start.3
  7.2 1.4 %copy-done = bf16[160,5120]{1,0:T(8,128)(2,1)S(1)} copy-done((bf16[160,5120]{1,0:T(8,128)(2,1)S(1)}, bf16[160,5120]{1,0:T(8,128)(2,1)}, u32[]{:S(2)}) %copy-start) | copy-done | bytes 1638424
  8.6 1.1 convolution_convert_fusion.3
  9.7 0.9 reshape.71
  10.6 5.2 %all-to-all-start.1 = ((bf16[8,4,5120]{2,1,0:T(4,128)(2,1)}), bf16[8,4,5120]{2,1,0:T(4,128)(2,1)S(1)}, u32[]{:S(2)}, u32[]{:S(2)}) async-start(bf16[8,4,5120]{2,1,0:T(4,128)(2,1)} %reshape.71), calls=%async_computation.1 | async-start | bytes 655360 | tf_op jit(solution)/shard_map/all_to_all | solution.py:74
  15.8 0.0 reduce-scatter.2.cloned.1.call-start
  15.8 0.0 copy-done.1
  15.8 0.1 fusion.6
  16.0 0.0 copy-done.3
  16.0 3.3 %convolution_convert_fusion.4 = bf16[128,1920]{1,0:T(8,128)(2,1)S(1)} fusion(bf16[1280,1920]{1,0:T(8,128)(2,1)} %param.13, bf16[128,1280]{1,0:T(8,128)(2,1)S(1)} %copy-done.1, f32[1280]{0:T(1024)S(1)} %copy-done.3, f32[128]{0:T(128)S(1)} %add_rsqrt_fusion), kind=kOutput, calls=%fused_computation.7 | convolution fusion | flops 630046720 | bytes 5740032 | tf_op jit(solution)/shard_map/dot_general | solution.py:23
  19.4 0.0 copy-start.6
  19.4 0.3 reshape.65
  19.7 0.3 reshape.66
  20.0 0.0 copy-done.6
  20.0 0.1 iota_compare_fusion.3
  20.1 1.1 fusion.4
  21.2 0.4 fusion.26
  21.6 0.3 reshape.64
  21.8 0.0 copy-start.5
  21.8 1.6 %fusion.5 = bf16[8,16,8,80]{3,1,2,0:T(8,128)(2,1)S(1)} fusion(bf16[8,16,8,80]{3,2,1,0:T(8,128)(2,1)S(1)} %reshape.64, f32[8,8,16]{2,1,0:T(8,128)S(1)} %fusion.26, f32[8,8,16,16]{2,3,1,0:T(8,128)} %fusion.4), kind=kOutput, calls=%fused_computation.13 | convolution fusion | flops 2753551 | bytes 397312 | tf_op jit(solution)/shard_map/nhqk,nkhd->nqhd/dot_general | solution.py:33
  23.4 0.1 copy.18
  23.5 0.2 reshape.67
  23.7 0.0 all-to-all-done.1
  23.7 0.1 copy.21
  23.8 0.0 copy-done.5
  23.8 0.3 convolution_convert_fusion
  24.1 0.2 reshape.73
  24.3 2.3 %fusion.31 = f32[640,1280]{1,0:T(8,128)} fusion(bf16[128,640]{1,0:T(8,128)(2,1)S(1)} %reshape.67, bf16[128,1280]{1,0:T(8,128)(2,1)S(1)} %reshape.73), kind=kOutput, calls=%fused_computation.38 | convolution fusion | flops 209715200 | bytes 3768320 | tf_op jit(solution)/shard_map/dot_general | solution.py:83
  26.6 0.0 reduce-scatter.2.cloned.1.call-update
  26.6 48.7 %reduce-scatter.2.cloned.1.call-done = f32[80,1280]{1,0:T(8,128)} async-done(((f32[640,1280]{1,0:T(8,128)}), f32[80,1280]{1,0:T(8,128)}) %reduce-scatter.2.cloned.1.call-update) | async-done | bytes 409616 | tf_op jit(solution)/shard_map/reduce_scatter | solution.py:82
  75.3 1.5 %collective-permute-start = (f32[80,1280]{1,0:T(8,128)}, f32[80,1280]{1,0:T(8,128)S(1)}, u32[]{:S(2)}, u32[]{:S(2)}) collective-permute-start(f32[80,1280]{1,0:T(8,128)} %reduce-scatter.2.cloned.1.call-done), channel_id=1, source_target_pairs={{0,1},{1,0},{2,3},{3,2},{4,5},{5,4},{6,7},{7,6},{8,9},{9,8},{10,11... | collective-permute-start | bytes 1228808 | tf_op jit(solution)/shard_map/ppermute | solution.py:92
  76.8 1.9 %fusion.1 = bf16[128,1280]{1,0:T(8,128)(2,1)S(1)} fusion(bf16[128,640]{1,0:T(8,128)(2,1)S(1)} %reshape.67, bf16[640,1280]{1,0:T(8,128)(2,1)} %param.14, bf16[128,1280]{1,0:T(8,128)(2,1)S(1)} %copy-done.1), kind=kOutput, calls=%fused_computation.6 | convolution fusion | flops 210206720 | bytes 2457600 | tf_op jit(solution)/shard_map/dot_general | solution.py:37
  78.7 0.0 copy-start.2
  78.7 0.2 reshape.68
  78.8 0.2 convolution_convert_fusion.1
  79.1 0.0 copy-start.4
  79.1 1.0 copy.19
  80.1 3.4 %all-to-all-start = ((bf16[8,4,5120]{2,1,0:T(4,128)(2,1)}), bf16[8,4,5120]{2,1,0:T(4,128)(2,1)S(1)}, u32[]{:S(2)}, u32[]{:S(2)}) async-start(bf16[8,4,5120]{2,1,0:T(4,128)(2,1)} %copy.19), calls=%async_computation | async-start | bytes 655360 | tf_op jit(solution)/shard_map/all_to_all | solution.py:64
  83.5 3.2 %collective-permute-done = f32[80,1280]{1,0:T(8,128)S(1)} collective-permute-done((f32[80,1280]{1,0:T(8,128)}, f32[80,1280]{1,0:T(8,128)S(1)}, u32[]{:S(2)}, u32[]{:S(2)}) %collective-permute-start) | collective-permute-done | bytes 409632 | tf_op jit(solution)/shard_map/ppermute | solution.py:92
  86.7 0.0 copy-done.2
  86.8 2.5 %collective-permute-start.1 = (f32[80,1280]{1,0:T(8,128)S(1)}, f32[80,1280]{1,0:T(8,128)S(1)}, u32[]{:S(2)}, u32[]{:S(2)}) collective-permute-start(f32[80,1280]{1,0:T(8,128)S(1)} %add.25), channel_id=1, source_target_pairs={{0,2},{1,3},{2,0},{3,1},{4,6},{5,7},{6,4},{7,5},{8,10},{9,11},{10,... | collective-permute-start | bytes 1228808 | tf_op jit(solution)/shard_map/ppermute | solution.py:92
  89.2 1.8 %all-to-all-done = bf16[8,4,5120]{2,1,0:T(4,128)(2,1)S(1)} async-done(((bf16[8,4,5120]{2,1,0:T(4,128)(2,1)}), bf16[8,4,5120]{2,1,0:T(4,128)(2,1)S(1)}, u32[]{:S(2)}, u32[]{:S(2)}) %all-to-all-start) | async-done | bytes 327712 | tf_op jit(solution)/shard_map/all_to_all | solution.py:64
  91.1 0.1 reshape.70
  91.2 1.8 %convolution_convert_fusion.2 = bf16[160,5120]{1,0:T(8,128)(2,1)} fusion(bf16[32,5120]{1,0:T(8,128)(2,1)S(1)} %reshape.70, s32[160]{0:T(256)S(1)} %copy-done.4), kind=kOutput, calls=%fused_computation.3 | convolution fusion | flops 53253120 | bytes 1966720 | tf_op jit(solution)/shard_map/dot_general | solution.py:65
  93.0 13.9 %collective-permute-done.1 = f32[80,1280]{1,0:T(8,128)S(1)} collective-permute-done((f32[80,1280]{1,0:T(8,128)S(1)}, f32[80,1280]{1,0:T(8,128)S(1)}, u32[]{:S(2)}, u32[]{:S(2)}) %collective-permute-start.1) | collective-permute-done | bytes 409632 | tf_op jit(solution)/shard_map/ppermute | solution.py:92
  106.8 0.8 add_multiply_fusion
  (4 shorter events, 0.1 us)
Async XLA Ops:
  7.2 1.4 %copy-start = (bf16[160,5120]{1,0:T(8,128)(2,1)S(1)}, bf16[160,5120]{1,0:T(8,128)(2,1)}, u32[]{:S(2)}) copy-start(bf16[160,5120]{1,0:T(8,128)(2,1)} %param.12) | copy-start | bytes 4915204
  7.2 8.7 %copy-start.1 = (bf16[128,1280]{1,0:T(8,128)(2,1)S(1)}, bf16[128,1280]{1,0:T(8,128)(2,1)}, u32[]{:S(2)}) copy-start(bf16[128,1280]{1,0:T(8,128)(2,1)} %param.8) | copy-start | bytes 983044
  7.2 8.8 %copy-start.3 = (f32[1280]{0:T(1024)S(1)}, f32[1280]{0:T(1024)}, u32[]{:S(2)}) copy-start(f32[1280]{0:T(1024)} %param.15) | copy-start | bytes 15364
  10.6 13.1 %all-to-all-start.1 = ((bf16[8,4,5120]{2,1,0:T(4,128)(2,1)}), bf16[8,4,5120]{2,1,0:T(4,128)(2,1)S(1)}, u32[]{:S(2)}, u32[]{:S(2)}) async-start(bf16[8,4,5120]{2,1,0:T(4,128)(2,1)} %reshape.71), calls=%async_computation.1 | async-start | bytes 655360 | tf_op jit(solution)/shard_map/all_to_all | solution.py:74
  15.8 59.5 %reduce-scatter.2.cloned.1.call-start = ((), (), s32[]{:S(2)}) async-start(), calls=%async_computation.3 | async-start | bytes 3686400 | tf_op jit(solution)/shard_map/reduce_scatter | solution.py:82
  19.4 0.7 copy-start.6
  21.8 2.0 %copy-start.5 = (s32[8]{0:T(128)S(1)}, s32[8]{0:T(128)}, u32[]{:S(2)}) copy-start(s32[8]{0:T(128)} %param.9) | copy-start | bytes 100
  75.3 11.4 %collective-permute-start = (f32[80,1280]{1,0:T(8,128)}, f32[80,1280]{1,0:T(8,128)S(1)}, u32[]{:S(2)}, u32[]{:S(2)}) collective-permute-start(f32[80,1280]{1,0:T(8,128)} %reduce-scatter.2.cloned.1.call-done), channel_id=1, source_target_pairs={{0,1},{1,0},{2,3},{3,2},{4,5},{5,4},{6,7},{7,6},{8,9},{9,8},{10,11... | collective-permute-start | bytes 1228808 | tf_op jit(solution)/shard_map/ppermute | solution.py:92
  78.7 8.1 %copy-start.2 = (f32[80,1280]{1,0:T(8,128)S(1)}, f32[80,1280]{1,0:T(8,128)}, u32[]{:S(2)}) copy-start(f32[80,1280]{1,0:T(8,128)} %reduce-scatter.2.cloned.1.call-done) | copy-start | bytes 1228804
  79.1 12.1 %copy-start.4 = (s32[160]{0:T(256)S(1)}, s32[160]{0:T(256)}, u32[]{:S(2)}) copy-start(s32[160]{0:T(256)} %param.11) | copy-start | bytes 1924
  80.1 11.0 %all-to-all-start = ((bf16[8,4,5120]{2,1,0:T(4,128)(2,1)}), bf16[8,4,5120]{2,1,0:T(4,128)(2,1)S(1)}, u32[]{:S(2)}, u32[]{:S(2)}) async-start(bf16[8,4,5120]{2,1,0:T(4,128)(2,1)} %copy.19), calls=%async_computation | async-start | bytes 655360 | tf_op jit(solution)/shard_map/all_to_all | solution.py:64
  86.8 20.1 %collective-permute-start.1 = (f32[80,1280]{1,0:T(8,128)S(1)}, f32[80,1280]{1,0:T(8,128)S(1)}, u32[]{:S(2)}, u32[]{:S(2)}) collective-permute-start(f32[80,1280]{1,0:T(8,128)S(1)} %add.25), channel_id=1, source_target_pairs={{0,2},{1,3},{2,0},{3,1},{4,6},{5,7},{6,4},{7,5},{8,10},{9,11},{10,... | collective-permute-start | bytes 1228808 | tf_op jit(solution)/shard_map/ppermute | solution.py:92
Sparse Core Ops, SparseCore 0:
  26.7 48.5 reduce-scatter.1
